TPU v7x, 256 devices: a whole 4x4x8 slice. The times are simulated.
256 devices in a mesh: orb: 64 (over x, z, core), aux: 4 (over y).
Axes of the slice: x: 4, y: 4, z: 8, core: 2. Of those that a mesh axis runs over, the one named last changes fastest.
Arguments:
- tensor: bfloat16 [30720, 2, 64, 256], P('aux', None, 'orb'), may hold values from -6 to 6
- density: bfloat16 [64, 512, 512], P('orb'), may hold values from -0.375 to 0.375
- block_ids: int32 [2, 64, 4], P(None, 'orb'), may hold values from 0 to 7
- counts: int32 [2, 64], P(None, 'orb'), may hold values from 1 to 4
Outputs:
- panel: float32 [64, 30720], P(None, ('aux', 'orb'))
All inputs are finite; a program needn't handle non-finite values.
Results may differ from a plain program's by a relative error of at most 0.0029.
Values may be sent and summed in bfloat16 or wider, within the bound.
A program may use at most 128 MiB of HBM per device.

v0:
```python
import math

import jax
import jax.numpy as jnp
from jax import lax
from jax.sharding import PartitionSpec as P

PANEL = 64


def spread(shard, axis, root):
    mine = lax.axis_index(axis) == root
    return lax.psum(jnp.where(mine, shard, jnp.zeros_like(shard)), axis)


def reduce_panel(panel_term):
    return lax.psum_scatter(panel_term, "orb", scatter_dimension=1, tiled=True)


def on_device(tensor, density, block_ids, counts):
    slab_count = tensor.shape[1]
    full_width = tensor.shape[3]
    slot_count = block_ids.shape[2]
    block_width = full_width // slot_count
    window_count = density.shape[1] // block_width
    live_slots = (
        lax.broadcasted_iota(jnp.int32, (slab_count, slot_count), 1) < counts[:, 0][:, None]
    )
    column_live = jnp.repeat(live_slots, block_width, axis=1)
    masked = jnp.where(column_live[None, :, :], tensor[:, :, 0, :], jnp.zeros((), jnp.bfloat16))
    tile_grid = (
        density[0].astype(jnp.float32).reshape(window_count, block_width, window_count, block_width)
    )
    selector = (
        block_ids[:, 0, :, None] == lax.broadcasted_iota(jnp.int32, (1, 1, window_count), 2)
    ).astype(jnp.float32)
    local_density = jnp.einsum(
        "ksw,wixj,ktx->ksitj", selector, tile_grid, selector, precision=lax.Precision.HIGHEST
    )
    local_density = local_density.reshape(slab_count, full_width, full_width).astype(jnp.bfloat16)
    mixed_rows = jnp.einsum(
        "rkc,kcd->rkd", masked, local_density, preferred_element_type=jnp.float32
    ).astype(jnp.bfloat16)
    factor = 1.0 / math.sqrt(slab_count * lax.axis_size("orb") * full_width)
    leading = spread(masked[:PANEL], "aux", 0)
    panel_sum = None
    for slab_index in range(slab_count):
        panel_term = lax.dot_general(
            leading[:, slab_index, :],
            mixed_rows[:, slab_index, :],
            (((1,), (1,)), ((), ())),
            preferred_element_type=jnp.float32,
        )
        reduced = reduce_panel(panel_term * factor)
        panel_sum = reduced if panel_sum is None else panel_sum + reduced
    return panel_sum


def solution(mesh):
    return jax.shard_map(
        on_device,
        mesh=mesh,
        in_specs=(
            P("aux", None, "orb", None),
            P("orb", None, None),
            P(None, "orb", None),
            P(None, "orb"),
        ),
        out_specs=P(None, ("aux", "orb")),
        check_vma=False,
    )
```

profile of v0, /device:TPU:16, one launch (start us, length us, event | category | flops | bytes accessed | tf_op | source)
XLA Modules:
  0.0 270.7 jit_solution(3410205117711670735)
XLA Ops:
  6.5 0.0 all-reduce.4.cloned.1.call-start
  6.5 0.7 iota_compare_fusion.1
  7.3 0.1 broadcast_in_dim.20
  7.3 0.1 broadcast_in_dim.21
  7.4 0.0 copy-start
  7.4 0.0 copy-start.2
  7.4 7.5 %bitcast_select_fusion = bf16[7680,2,256]{2,0,1:T(8,128)(2,1)} fusion(bf16[7680,2,1,256]{3,1,2,0:T(2,128)(2,1)} %param.4, pred[2,256]{1,0:T(4,128)(4,1)S(1)} %broadcast_in_dim.21), kind=kLoop, calls=%fused_computation.4 | loop fusion | flops 3932160 | bytes 15729152 | tf_op jit(solution)/shard_map/jit(_where)/select_n | solution.py:30
  14.9 1.5 slice_select_fusion
  16.4 0.0 all-reduce.4.cloned.1.call-update
  16.4 0.0 all-reduce.6.cloned.1.call-start
  16.4 0.0 copy-done
  16.5 0.5 reshape.8
  17.0 0.0 copy-done.2
  17.0 0.9 convolution_bitcast_fusion
  17.9 1.1 fusion.8
  19.0 0.2 copy.12
  19.2 0.3 reshape.12
  19.5 8.6 %fusion = bf16[7680,2,256]{0,2,1:T(8,128)(2,1)} fusion(bf16[2,256,256]{2,1,0:T(8,128)(2,1)S(1)} %reshape.12, bf16[7680,2,256]{2,0,1:T(8,128)(2,1)} %bitcast_select_fusion), kind=kOutput, calls=%fused_computation.1 | convolution fusion | flops 2017198080 | bytes 15990784 | tf_op jit(solution)/shard_map/rkc,kcd->rkd/dot_general | solution.py:41
  28.1 36.3 %all-reduce.4.cloned.1.call-done = bf16[64,2,256]{2,0,1:T(8,128)(2,1)} async-done(((bf16[64,2,256]{2,0,1:T(8,128)(2,1)}), bf16[64,2,256]{2,0,1:T(8,128)(2,1)}) %all-reduce.4.cloned.1.call-update) | async-done | bytes 65552 | tf_op jit(solution)/shard_map/psum | solution.py:13
  64.4 0.0 copy-start.1
  64.4 3.0 %fusion.2 = f32[64,7680]{1,0:T(8,128)S(1)} fusion(bf16[7680,2,256]{0,2,1:T(8,128)(2,1)} %fusion, bf16[64,2,256]{2,0,1:T(8,128)(2,1)} %all-reduce.4.cloned.1.call-done), kind=kOutput, calls=%fused_computation.7 | convolution fusion | flops 251658240 | bytes 5931008 | tf_op jit(solution)/shard_map/dot_general | solution.py:48
  67.4 0.0 copy-done.1
  67.4 0.0 copy-start.3
  67.4 4.3 %fusion.1 = f32[64,7680]{1,0:T(8,128)} fusion(f32[64,7680]{1,0:T(8,128)S(1)} %fusion.2, bf16[7680,2,256]{0,2,1:T(8,128)(2,1)} %fusion, bf16[64,2,256]{2,0,1:T(8,128)(2,1)S(1)} %copy-done.1), kind=kOutput, calls=%fused_computation.3 | convolution fusion | flops 252641280 | bytes 7897088 | tf_op jit(solution)/shard_map/dot_general | solution.py:48
  71.7 0.0 all-reduce.6.cloned.1.call-update
  71.8 0.0 copy-done.3
  71.8 0.6 dynamic-slice
  73.0 189.3 %all-reduce.6.cloned.1.call-done = f32[64,7680]{1,0:T(8,128)} async-done(((f32[64,7680]{1,0:T(8,128)}), f32[64,7680]{1,0:T(8,128)}) %all-reduce.6.cloned.1.call-update) | async-done | bytes 1966096
  262.3 1.5 constant_dynamic-slice_fusion
Async XLA Ops:
  6.5 57.9 %all-reduce.4.cloned.1.call-start = ((), (), s32[]{:S(2)}) async-start(), calls=%async_computation | async-start | bytes 131072 | tf_op jit(solution)/shard_map/psum | solution.py:13
  7.4 9.0 %copy-start = (bf16[1,512,512]{2,1,0:T(8,128)(2,1)S(1)}, bf16[1,512,512]{2,1,0:T(8,128)(2,1)}, u32[]{:S(2)}) copy-start(bf16[1,512,512]{2,1,0:T(8,128)(2,1)} %param.5) | copy-start | bytes 1572868
  7.4 9.6 %copy-start.2 = (s32[2,1,4]{2,1,0:T(1,128)S(1)}, s32[2,1,4]{2,1,0:T(1,128)}, u32[]{:S(2)}) copy-start(s32[2,1,4]{2,1,0:T(1,128)} %param.6) | copy-start | bytes 100
  16.4 245.9 %all-reduce.6.cloned.1.call-start = ((), (), s32[]{:S(2)}) async-start(), calls=%async_computation.1 | async-start | bytes 3932160
  64.4 3.0 %copy-start.1 = (bf16[64,2,256]{2,0,1:T(8,128)(2,1)S(1)}, bf16[64,2,256]{2,0,1:T(8,128)(2,1)}, u32[]{:S(2)}) copy-start(bf16[64,2,256]{2,0,1:T(8,128)(2,1)} %all-reduce.4.cloned.1.call-done) | copy-start | bytes 196612
  67.4 4.4 %copy-start.3 = (u32[256]{0:T(256)S(1)}, u32[256]{0:T(256)}, u32[]{:S(2)}) copy-start(u32[256]{0:T(256)} %constant.17) | copy-start | bytes 3076
Sparse Core Ops, SparseCore 0:
  16.5 47.8 all-reduce.3
  71.9 190.4 all-reduce.5
where the time goes:
time: 271 us
  waiting for transfers between devices  226 us (83%)
  matrix products  17.8 us (7%)
  between operations  14.1 us (5%)
  other arithmetic  9.66 us (4%)
  local copies, waits for them, and re-layouts  3.35 us (1%)
    unnamed x3, waiting for transfers between devices  189 us
    psum x1, waiting for transfers between devices, spread(): return lax.psum(jnp.where(mine, shard, jnp.zeros_like(shard)), axis)  36.3 us
    dot_general x1, matrix products, on_device(): jnp.einsum('rkc,kcd->rkd', masked, local_density, preferred_element_type=...  8.56 us
    select_n x1, other arithmetic, on_device(): jnp.where(column_live[None, :, :], tensor[:, :, 0, :], jnp.zeros((), jnp....  7.46 us
    dot_general x2, matrix products, on_device(): lax.dot_general(leading[:, slab_index, :], mixed_rows[:, slab_index, :],...  7.28 us
  transfers between devices with their start and end apart: 2, of which 2 were waited for; matrix products, arithmetic and copies ran while one was open for 5% of the time, Pallas kernels for 0%

commit v1 on v0

v1 whole, which is shorter than its diff:
```python
import functools
import math

import jax
import jax.numpy as jnp
from jax import lax
from jax.experimental import pallas as pl
from jax.experimental.pallas import tpu as pltpu
from jax.sharding import PartitionSpec as P

PANEL = 64
NX, NZ, NC, NAUX = 4, 8, 2, 4
SLABS = 2
SLOTS = 4
BLK = 64
WIDTH = SLOTS * BLK
WINDOW = 512
ROWS = 120
PAIR = NC * ROWS
TILE = 64
SHIFT = ROWS - TILE
Z_ORDER = (4, 3, 5, 2, 6, 1, 7, 0)
GROUPS = len(Z_ORDER)
X_LAG = 3
F32, BF16 = jnp.float32, jnp.bfloat16
NT = (((1,), (1,)), ((), ()))


def kernel(
    tensor, density, block_ids, counts, out,
    rows, dens, lead, weights, product, own, sibling_out, sibling_in, x_out, x_in, z_out, z_in,
    rows_sem, dens_sem, lead_sem, lead_send, lead_recv,
    c_send, c_recv, x_send, x_recv, z_send, z_recv,
):
    orb, aux = lax.axis_index("orb"), lax.axis_index("aux")
    core = lax.rem(orb, NC)
    z = lax.rem(orb // NC, NZ)
    x = orb // (NC * NZ)

    def at(x_of, z_of, core_of):
        return (x_of * NZ + z_of) * NC + core_of

    sibling = {"orb": at(x, z, 1 - core)}
    x_peer = [{"orb": at(lax.rem(x + d, NX), z, core)} for d in range(NX)]
    z_peer = [{"orb": at(x, lax.rem(z + d, NZ), core)} for d in range(NZ)]

    barrier = pltpu.get_barrier_semaphore()
    for peer in [sibling] + x_peer[1:] + z_peer[1:]:
        pl.semaphore_signal(barrier, inc=1, device_id=peer, device_id_type=pl.DeviceIdType.MESH)

    @pl.when(aux == 0)
    def _():
        for d in range(1, NAUX):
            pl.semaphore_signal(barrier, inc=1, device_id={"aux": d}, device_id_type=pl.DeviceIdType.MESH)

    @pl.when(aux != 0)
    def _():
        pl.semaphore_signal(barrier, inc=1, device_id={"aux": 0}, device_id_type=pl.DeviceIdType.MESH)

    lead_in = [
        pltpu.make_async_copy(
            tensor.at[0, 0, pl.ds(0, PANEL), :, pl.ds(128 * j, 128)], lead.at[j], lead_sem.at[j]
        )
        for j in range(2)
    ]

    @pl.when(aux == 0)
    def _():
        for copy in lead_in:
            copy.start()

    dens_in = pltpu.make_async_copy(density.at[0], dens, dens_sem)
    dens_in.start()
    rows_in = [
        [
            pltpu.make_async_copy(
                tensor.at[:, lax.rem(z + dz, NZ), :, :, pl.ds(128 * j, 128)],
                rows.at[g, j],
                rows_sem.at[g, j],
            )
            for j in range(2)
        ]
        for g, dz in enumerate(Z_ORDER)
    ]
    for pair in rows_in:
        for copy in pair:
            copy.start()

    def lead_copy(d, j):
        return pltpu.make_async_remote_copy(
            src_ref=lead.at[j], dst_ref=lead.at[j],
            send_sem=lead_send.at[d - 1, j], recv_sem=lead_recv.at[j],
            device_id={"aux": d}, device_id_type=pl.DeviceIdType.MESH,
        )

    @pl.when(aux == 0)
    def _():
        pl.semaphore_wait(barrier, 1 + NX - 1 + NZ - 1 + NAUX - 1)
        for j in range(2):
            lead_in[j].wait()
            for d in range(1, NAUX):
                lead_copy(d, j).start()

    @pl.when(aux != 0)
    def _():
        pl.semaphore_wait(barrier, 1 + NX - 1 + NZ - 1 + 1)

    dens_in.wait()
    locals_ = []

    def picks(k, shape, axis):
        column = lax.broadcasted_iota(jnp.int32, shape, axis)
        slot = column // BLK
        target = jnp.zeros(shape, jnp.int32)
        for s in range(SLOTS):
            target = jnp.where(slot == s, jnp.full(shape, block_ids[k, 0, s] * BLK), target)
        target = jnp.where(slot < jnp.full(shape, counts[0, k]), target + lax.rem(column, BLK), -1)
        window = lax.broadcasted_iota(jnp.int32, (WINDOW, WIDTH) if axis else (WIDTH, WINDOW), 1 - axis)
        return jnp.where(window == target, 1.0, 0.0).astype(BF16)

    for k in range(SLABS):
        some_rows = jnp.dot(picks(k, (WIDTH, 1), 0), dens[...], preferred_element_type=F32).astype(BF16)
        block = jnp.dot(some_rows, picks(k, (1, WIDTH), 1), preferred_element_type=F32)
        locals_.append(block.astype(BF16))

    @pl.when(aux != 0)
    def _():
        for j in range(2):
            lead_copy(1, j).wait_recv()

    leading = jnp.concatenate([lead[j].reshape(SLABS * PANEL, 128) for j in range(2)], axis=1)
    a = lax.broadcasted_iota(jnp.int32, (SLABS * PANEL, SLABS * PANEL), 0)
    b = lax.broadcasted_iota(jnp.int32, (SLABS * PANEL, SLABS * PANEL), 1)
    weight = None
    for k in range(SLABS):
        sort = jnp.where((b == SLABS * (a - k * PANEL) + k) & (a // PANEL == k), 1.0, 0.0).astype(BF16)
        chosen = jnp.dot(sort, leading, preferred_element_type=F32).astype(BF16)
        term = lax.dot_general(locals_[k], chosen, NT, preferred_element_type=F32)
        weight = term if weight is None else weight + term
    high = weight.astype(BF16)
    weights[:, : SLABS * PANEL] = high
    weights[:, SLABS * PANEL :] = (weight - high.astype(F32)).astype(BF16)

    left = lax.broadcasted_iota(jnp.int32, (TILE, 128), 1) < PANEL

    def multiply(g):
        for j in range(2):
            rows_in[g][j].wait()
        for d in range(NX):
            x_of = lax.rem(x + d, NX)
            slot_of = (g * NX + d) % 2
            strip = jnp.concatenate(
                [rows[g, j, x_of].reshape(SLABS * PAIR, 128) for j in range(2)], axis=1
            )
            y = jnp.dot(strip, weights[...], preferred_element_type=F32)
            product[slot_of] = y[:, :128] + y[:, 128:]
            for core_of, dest in ((1 - core, sibling_out), (core, own)):
                start = core_of * (SLABS * ROWS)

                def every_second(offset):
                    return product[slot_of, pl.ds(start + offset, TILE, SLABS), :]

                low = [every_second(k) for k in range(SLABS)]
                top = [every_second(SLABS * SHIFT + k) for k in range(SLABS)]
                dest[g, d] = jnp.where(left, low[0], top[1]) + pltpu.roll(
                    jnp.where(left, top[0], low[1]), PANEL, 1
                )

    def core_copy(g):
        return pltpu.make_async_remote_copy(
            src_ref=sibling_out.at[g], dst_ref=sibling_in.at[g],
            send_sem=c_send.at[g], recv_sem=c_recv.at[g],
            device_id=sibling, device_id_type=pl.DeviceIdType.MESH,
        )

    def x_copy(g, d):
        return pltpu.make_async_remote_copy(
            src_ref=x_out.at[g, d - 1], dst_ref=x_in.at[g, d - 1],
            send_sem=x_send.at[g, d - 1], recv_sem=x_recv.at[g, d - 1],
            device_id=x_peer[d], device_id_type=pl.DeviceIdType.MESH,
        )

    def z_copy(g):
        return pltpu.make_async_remote_copy(
            src_ref=z_out.at[g], dst_ref=z_in.at[g],
            send_sem=z_send.at[g], recv_sem=z_recv.at[g],
            device_id=z_peer[Z_ORDER[g]], device_id_type=pl.DeviceIdType.MESH,
        )

    def add_sibling(g):
        core_copy(g).wait_recv()
        for d in (2, 1, 3):
            x_out[g, d - 1] = (own[g, d] + sibling_in[g, d]).astype(BF16)
            x_copy(g, d).start()

    def add_x(g):
        total = own[g, 0] + sibling_in[g, 0]
        for d in (1, 3, 2):
            x_copy(g, d).wait_recv()
            total = total + x_in[g, d - 1].astype(F32)
        if g < GROUPS - 1:
            z_out[g] = total.astype(BF16)
            z_copy(g).start()
        return total

    for g in range(GROUPS):
        multiply(g)
        core_copy(g).start()
        if g >= 1:
            add_sibling(g - 1)
        if g >= X_LAG:
            add_x(g - X_LAG)
    add_sibling(GROUPS - 1)
    for g in range(GROUPS - X_LAG, GROUPS):
        total = add_x(g)
    for g in range(GROUPS - 1):
        z_copy(g).wait_recv()
        total = total + z_in[g].astype(F32)
    total = total * (1.0 / math.sqrt(SLABS * NX * NZ * NC * WIDTH))
    turned = total.T
    out[:, :TILE] = turned[:PANEL]
    out[:, TILE:] = turned[PANEL:, TILE - SHIFT :]

    for g in range(GROUPS):
        core_copy(g).wait_send()
        for d in range(1, NX):
            x_copy(g, d).wait_send()
        if g < GROUPS - 1:
            z_copy(g).wait_send()

    @pl.when(aux == 0)
    def _():
        for j in range(2):
            for d in range(1, NAUX):
                lead_copy(d, j).wait_send()


def on_device(tensor, density, block_ids, counts):
    tensor = tensor.reshape(NX, NZ, PAIR, SLABS, WIDTH)
    piece = (TILE, 128)
    return pl.pallas_call(
        kernel,
        out_shape=jax.ShapeDtypeStruct((PANEL, ROWS), F32),
        in_specs=[
            pl.BlockSpec(memory_space=pltpu.HBM),
            pl.BlockSpec(memory_space=pltpu.HBM),
            pl.BlockSpec(memory_space=pltpu.SMEM),
            pl.BlockSpec(memory_space=pltpu.SMEM),
        ],
        out_specs=pl.BlockSpec(memory_space=pltpu.VMEM),
        scratch_shapes=[
            pltpu.VMEM((GROUPS, 2, NX, PAIR, SLABS, 128), BF16),
            pltpu.VMEM((WINDOW, WINDOW), BF16),
            pltpu.VMEM((2, PANEL, SLABS, 128), BF16),
            pltpu.VMEM((WIDTH, 2 * SLABS * PANEL), BF16),
            pltpu.VMEM((2, SLABS * PAIR, 128), F32),
            pltpu.VMEM((GROUPS, NX) + piece, F32),
            pltpu.VMEM((GROUPS, NX) + piece, F32),
            pltpu.VMEM((GROUPS, NX) + piece, F32),
            pltpu.VMEM((GROUPS, NX - 1) + piece, BF16),
            pltpu.VMEM((GROUPS, NX - 1) + piece, BF16),
            pltpu.VMEM((GROUPS - 1,) + piece, BF16),
            pltpu.VMEM((GROUPS - 1,) + piece, BF16),
            pltpu.SemaphoreType.DMA((GROUPS, 2)),
            pltpu.SemaphoreType.DMA,
            pltpu.SemaphoreType.DMA((2,)),
            pltpu.SemaphoreType.DMA((NAUX - 1, 2)),
            pltpu.SemaphoreType.DMA((2,)),
            pltpu.SemaphoreType.DMA((GROUPS,)),
            pltpu.SemaphoreType.DMA((GROUPS,)),
            pltpu.SemaphoreType.DMA((GROUPS, NX - 1)),
            pltpu.SemaphoreType.DMA((GROUPS, NX - 1)),
            pltpu.SemaphoreType.DMA((GROUPS - 1,)),
            pltpu.SemaphoreType.DMA((GROUPS - 1,)),
        ],
        compiler_params=pltpu.CompilerParams(
            collective_id=0, has_side_effects=True, vmem_limit_bytes=60 << 20
        ),
    )(tensor, density, block_ids, counts.T)


def solution(mesh):
    return jax.shard_map(
        on_device,
        mesh=mesh,
        in_specs=(
            P("aux", None, "orb", None),
            P("orb", None, None),
            P(None, "orb", None),
            P(None, "orb"),
        ),
        out_specs=P(None, ("aux", "orb")),
        check_vma=False,
    )
```

time: 271 us -> 33.4 us (0.12)
  waiting for transfers between devices: 226 us -> 0 us
  Pallas kernels: 0 us -> 31.9 us
  matrix products: 17.8 us -> 0 us
  between operations: 14.1 us -> 0.01 us
  other arithmetic: 9.66 us -> 0 us
    unnamed x3 -> x0, waiting for transfers between devices: 189 us -> none
    psum x1 -> x0, waiting for transfers between devices: 36.3 us -> none  [spread(): return lax.psum(jnp.where(mine, shard, jnp.zeros_like(shard)), axis)]
    pallas_call x0 -> x1, Pallas kernels: none -> 31.9 us  [on_device(): pl.pallas_call(kernel, out_shape=jax.ShapeDtypeStruct((PANEL, ROWS), F32)...]
    dot_general x5 -> x0, matrix products: 17.8 us -> none  [the longest x1 8.56 us: on_device(): jnp.einsum('rkc,kcd->rkd', masked, local_density, preferred_element_type=...]
    select_n x2 -> x0, other arithmetic: 8.93 us -> none  [the longest x1 7.46 us: on_device(): jnp.where(column_live[None, :, :], tensor[:, :, 0, :], jnp.zeros((), jnp....]
  transfers between devices with their start and end apart: 2 -> 0, of which waited for: 2 -> 0; matrix products, arithmetic and copies ran while one was open for 5% -> 0% of each run, Pallas kernels for 0% -> 0%
where the time goes in v1:
time: 33.4 us; the launch traced here: 33.2 us
  Pallas kernels  31.9 us (96%)
  local copies, waits for them, and re-layouts  1.38 us (4%)
    pallas_call x1, Pallas kernels, on_device(): pl.pallas_call(kernel, out_shape=jax.ShapeDtypeStruct((PANEL, ROWS), F32)...  31.9 us
    unnamed x1, local copies, waits for them, and re-layouts  1.38 us

profile of v1, /device:TPU:16, one launch (start us, length us, event | category | flops | bytes accessed | tf_op | source)
XLA Modules:
  0.0 33.2 jit_solution(15607508670805067939)
XLA Ops:
  0.0 31.9 %shard_map.46 = f32[64,120]{1,0:T(8,128)} custom-call(bf16[4,8,240,2,256]{4,3,2,1,0:T(2,128)(2,1)} %bitcast.2, bf16[1,512,512]{2,1,0:T(8,128)(2,1)} %density.1, s32[2,1,4]{2,1,0:T(1,128)} %block_ids.1, s32[1,2]{1,0:T(1,128)} %bitcast.3), custom_call_target="tpu_custom_call" | custom-call | tf_op jit(solution)/shard_map/pallas_call | solution.py:241
  31.9 1.4 %copy.6 = f32[64,120]{1,0:T(8,128)} copy(f32[64,120]{1,0:T(8,128)} %shard_map.46) | data formatting | bytes 61440

commit v2 on v1

--- a/solution.py
+++ b/solution.py
@@ -21,13 +21,13 @@
 SHIFT = ROWS - TILE
 Z_ORDER = (4, 3, 5, 2, 6, 1, 7, 0)
 GROUPS = len(Z_ORDER)
-X_LAG = 3
+C_LAG, X_LAG = 2, 8
 F32, BF16 = jnp.float32, jnp.bfloat16
 NT = (((1,), (1,)), ((), ()))
 
 
 def kernel(
-    tensor, density, block_ids, counts, out,
+    tensor, density, block_ids_in, counts_in, out, block_ids, counts, small_sem,
     rows, dens, lead, weights, product, own, sibling_out, sibling_in, x_out, x_in, z_out, z_in,
     rows_sem, dens_sem, lead_sem, lead_send, lead_recv,
     c_send, c_recv, x_send, x_recv, z_send, z_recv,
@@ -69,6 +69,12 @@
         for copy in lead_in:
             copy.start()
 
+    small_in = [
+        pltpu.make_async_copy(block_ids_in, block_ids, small_sem.at[0]),
+        pltpu.make_async_copy(counts_in, counts, small_sem.at[1]),
+    ]
+    for copy in small_in:
+        copy.start()
     dens_in = pltpu.make_async_copy(density.at[0], dens, dens_sem)
     dens_in.start()
     rows_in = [
@@ -98,13 +104,16 @@
         pl.semaphore_wait(barrier, 1 + NX - 1 + NZ - 1 + NAUX - 1)
         for j in range(2):
             lead_in[j].wait()
-            for d in range(1, NAUX):
+        for d in (3, 1, 2):
+            for j in range(2):
                 lead_copy(d, j).start()
 
     @pl.when(aux != 0)
     def _():
         pl.semaphore_wait(barrier, 1 + NX - 1 + NZ - 1 + 1)
 
+    for copy in small_in:
+        copy.wait()
     dens_in.wait()
     locals_ = []
 
@@ -206,11 +215,12 @@
     for g in range(GROUPS):
         multiply(g)
         core_copy(g).start()
-        if g >= 1:
-            add_sibling(g - 1)
+        if g >= C_LAG:
+            add_sibling(g - C_LAG)
         if g >= X_LAG:
             add_x(g - X_LAG)
-    add_sibling(GROUPS - 1)
+    for g in range(GROUPS - C_LAG, GROUPS):
+        add_sibling(g)
     for g in range(GROUPS - X_LAG, GROUPS):
         total = add_x(g)
     for g in range(GROUPS - 1):
@@ -244,11 +254,14 @@
         in_specs=[
             pl.BlockSpec(memory_space=pltpu.HBM),
             pl.BlockSpec(memory_space=pltpu.HBM),
-            pl.BlockSpec(memory_space=pltpu.SMEM),
-            pl.BlockSpec(memory_space=pltpu.SMEM),
+            pl.BlockSpec(memory_space=pltpu.HBM),
+            pl.BlockSpec(memory_space=pltpu.HBM),
         ],
         out_specs=pl.BlockSpec(memory_space=pltpu.VMEM),
         scratch_shapes=[
+            pltpu.SMEM((SLABS, 1, SLOTS), jnp.int32),
+            pltpu.SMEM((1, SLABS), jnp.int32),
+            pltpu.SemaphoreType.DMA((2,)),
             pltpu.VMEM((GROUPS, 2, NX, PAIR, SLABS, 128), BF16),
             pltpu.VMEM((WINDOW, WINDOW), BF16),
             pltpu.VMEM((2, PANEL, SLABS, 128), BF16),
@@ -274,9 +287,9 @@
             pltpu.SemaphoreType.DMA((GROUPS - 1,)),
         ],
         compiler_params=pltpu.CompilerParams(
-            collective_id=0, has_side_effects=True, vmem_limit_bytes=60 << 20
+            collective_id=0, has_side_effects=True, vmem_limit_bytes=32 << 20
         ),
-    )(tensor, density, block_ids, counts.T)
+    )(*[pltpu.with_memory_space_constraint(a, pltpu.HBM) for a in (tensor, density, block_ids, counts.T)])
 
 
 def solution(mesh):

time: 33.4 us -> 28.2 us (0.84)
  Pallas kernels: 31.9 us -> 27.5 us
  local copies, waits for them, and re-layouts: 1.38 us -> 0.62 us
    pallas_call x1, Pallas kernels: 31.9 us -> 27.5 us  [on_device(): pl.pallas_call(kernel, out_shape=jax.ShapeDtypeStruct((PANEL, ROWS), F32)...]
    unnamed x1, local copies, waits for them, and re-layouts: 1.38 us -> 0.62 us
where the time goes in v2:
time: 28.2 us; the launch traced here: 28.1 us
  Pallas kernels  27.5 us (98%)
  local copies, waits for them, and re-layouts  0.62 us (2%)
    pallas_call x1, Pallas kernels, on_device(): pl.pallas_call(kernel, out_shape=jax.ShapeDtypeStruct((PANEL, ROWS), F32)...  27.5 us
    unnamed x1, local copies, waits for them, and re-layouts  0.62 us

profile of v2, /device:TPU:16, one launch (start us, length us, event | category | flops | bytes accessed | tf_op | source)
XLA Modules:
  0.0 28.1 jit_solution(16864356492904041822)
XLA Ops:
  0.0 27.5 %shard_map.46 = f32[64,120]{1,0:T(8,128)S(1)} custom-call(bf16[4,8,240,2,256]{4,3,2,1,0:T(2,128)(2,1)} %bitcast.2, bf16[1,512,512]{2,1,0:T(8,128)(2,1)} %density.1, s32[2,1,4]{2,1,0:T(1,128)} %block_ids_in.1, s32[1,2]{1,0:T(1,128)} %bitcast.3), custom_call_target="tpu_custom_call" | custom-call | tf_op jit(solution)/shard_map/pallas_call | solution.py:251
  27.5 0.6 %copy.6 = f32[64,120]{1,0:T(8,128)} copy(f32[64,120]{1,0:T(8,128)S(1)} %shard_map.46) | data formatting | bytes 61440

commit v3 on v2

--- a/solution.py
+++ b/solution.py
@@ -19,18 +19,18 @@
 PAIR = NC * ROWS
 TILE = 64
 SHIFT = ROWS - TILE
-Z_ORDER = (4, 3, 5, 2, 6, 1, 7, 0)
-GROUPS = len(Z_ORDER)
-C_LAG, X_LAG = 2, 8
+GROUPS = NZ
+BLOCKS = ((0,), (1,), (2,), (3,), (4,), (5,), (6,), (7,))
+C_LAG, X_LAG = 2, 4
 F32, BF16 = jnp.float32, jnp.bfloat16
 NT = (((1,), (1,)), ((), ()))
 
 
 def kernel(
     tensor, density, block_ids_in, counts_in, out, block_ids, counts, small_sem,
-    rows, dens, lead, weights, product, own, sibling_out, sibling_in, x_out, x_in, z_out, z_in,
+    rows, dens, lead, weights, product, own, sibling_out, sibling_in, x_out, x_in, totals, z_out, z_in,
     rows_sem, dens_sem, lead_sem, lead_send, lead_recv,
-    c_send, c_recv, x_send, x_recv, z_send, z_recv,
+    z_ready, c_send, c_recv, x_send, x_recv, z_send, z_recv,
 ):
     orb, aux = lax.axis_index("orb"), lax.axis_index("aux")
     core = lax.rem(orb, NC)
@@ -42,11 +42,15 @@
 
     sibling = {"orb": at(x, z, 1 - core)}
     x_peer = [{"orb": at(lax.rem(x + d, NX), z, core)} for d in range(NX)]
-    z_peer = [{"orb": at(x, lax.rem(z + d, NZ), core)} for d in range(NZ)]
+    z_peer = [{"orb": at(x, of, core)} for of in range(NZ)]
 
     barrier = pltpu.get_barrier_semaphore()
-    for peer in [sibling] + x_peer[1:] + z_peer[1:]:
+    for peer in [sibling] + x_peer[1:]:
         pl.semaphore_signal(barrier, inc=1, device_id=peer, device_id_type=pl.DeviceIdType.MESH)
+    for of in range(1, NZ):
+        @pl.when(z < of)
+        def _():
+            pl.semaphore_signal(barrier, inc=1, device_id=z_peer[of], device_id_type=pl.DeviceIdType.MESH)
 
     @pl.when(aux == 0)
     def _():
@@ -80,13 +84,13 @@
     rows_in = [
         [
             pltpu.make_async_copy(
-                tensor.at[:, lax.rem(z + dz, NZ), :, :, pl.ds(128 * j, 128)],
+                tensor.at[:, g, :, :, pl.ds(128 * j, 128)],
                 rows.at[g, j],
                 rows_sem.at[g, j],
             )
             for j in range(2)
         ]
-        for g, dz in enumerate(Z_ORDER)
+        for g in range(GROUPS)
     ]
     for pair in rows_in:
         for copy in pair:
@@ -101,16 +105,21 @@
 
     @pl.when(aux == 0)
     def _():
-        pl.semaphore_wait(barrier, 1 + NX - 1 + NZ - 1 + NAUX - 1)
+        pl.semaphore_wait(barrier, 1 + NX - 1 + NAUX - 1 + z)
         for j in range(2):
             lead_in[j].wait()
-        for d in (3, 1, 2):
+        for d in (2, 1, 3):
             for j in range(2):
                 lead_copy(d, j).start()
 
     @pl.when(aux != 0)
     def _():
-        pl.semaphore_wait(barrier, 1 + NX - 1 + NZ - 1 + 1)
+        pl.semaphore_wait(barrier, 1 + NX - 1 + 1 + z)
+
+    for of in range(NZ - 1):
+        @pl.when(z > of)
+        def _():
+            pl.semaphore_signal(z_ready.at[z], inc=1, device_id=z_peer[of], device_id_type=pl.DeviceIdType.MESH)
 
     for copy in small_in:
         copy.wait()
@@ -153,11 +162,9 @@
     left = lax.broadcasted_iota(jnp.int32, (TILE, 128), 1) < PANEL
 
     def multiply(g):
-        for j in range(2):
-            rows_in[g][j].wait()
         for d in range(NX):
             x_of = lax.rem(x + d, NX)
-            slot_of = (g * NX + d) % 2
+            slot_of = (g * NX + d) % 4
             strip = jnp.concatenate(
                 [rows[g, j, x_of].reshape(SLABS * PAIR, 128) for j in range(2)], axis=1
             )
@@ -189,43 +196,65 @@
             device_id=x_peer[d], device_id_type=pl.DeviceIdType.MESH,
         )
 
-    def z_copy(g):
+    def z_copy(g, slot):
         return pltpu.make_async_remote_copy(
-            src_ref=z_out.at[g], dst_ref=z_in.at[g],
-            send_sem=z_send.at[g], recv_sem=z_recv.at[g],
-            device_id=z_peer[Z_ORDER[g]], device_id_type=pl.DeviceIdType.MESH,
-        )
+            src_ref=z_out.at[g], dst_ref=z_in.at[slot],
+            send_sem=z_send.at[g], recv_sem=z_recv.at[slot],
+            device_id={"orb": at(x, g, core)}, device_id_type=pl.DeviceIdType.MESH,
+        )
+
+    def z_slot(g):
+        return lax.rem(z - g + 2 * NZ - 1, NZ)
 
     def add_sibling(g):
-        core_copy(g).wait_recv()
-        for d in (2, 1, 3):
+        for d in range(1, NX):
             x_out[g, d - 1] = (own[g, d] + sibling_in[g, d]).astype(BF16)
-            x_copy(g, d).start()
 
     def add_x(g):
         total = own[g, 0] + sibling_in[g, 0]
         for d in (1, 3, 2):
             x_copy(g, d).wait_recv()
             total = total + x_in[g, d - 1].astype(F32)
-        if g < GROUPS - 1:
-            z_out[g] = total.astype(BF16)
-            z_copy(g).start()
-        return total
-
-    for g in range(GROUPS):
-        multiply(g)
-        core_copy(g).start()
-        if g >= C_LAG:
-            add_sibling(g - C_LAG)
-        if g >= X_LAG:
-            add_x(g - X_LAG)
-    for g in range(GROUPS - C_LAG, GROUPS):
-        add_sibling(g)
-    for g in range(GROUPS - X_LAG, GROUPS):
-        total = add_x(g)
-    for g in range(GROUPS - 1):
-        z_copy(g).wait_recv()
-        total = total + z_in[g].astype(F32)
+        totals[g] = total
+        z_out[g] = total.astype(BF16)
+
+        @pl.when(z < g)
+        def _():
+            pl.semaphore_wait(z_ready.at[g], 1)
+
+        @pl.when(z != g)
+        def _():
+            z_copy(g, z_slot(g)).start()
+
+    for pair in rows_in:
+        for copy in pair:
+            copy.wait()
+    for step in range(len(BLOCKS) + C_LAG + X_LAG):
+        fresh = BLOCKS[step] if step < len(BLOCKS) else ()
+        ripe = BLOCKS[step - C_LAG] if 0 <= step - C_LAG < len(BLOCKS) else ()
+        done = BLOCKS[step - C_LAG - X_LAG] if step >= C_LAG + X_LAG else ()
+        for g in ripe:
+            core_copy(g).wait_recv()
+        for g in ripe:
+            add_sibling(g)
+        if not fresh:
+            for g in ripe:
+                for d in (2, 1, 3):
+                    x_copy(g, d).start()
+        for g in fresh:
+            multiply(g)
+        if fresh:
+            for g in ripe:
+                for d in (2, 1, 3):
+                    x_copy(g, d).start()
+        for g in fresh:
+            core_copy(g).start()
+        for g in done:
+            add_x(g)
+    total = totals[z]
+    for slot in range(NZ - 1):
+        z_copy(0, slot).wait_recv()
+        total = total + z_in[slot].astype(F32)
     total = total * (1.0 / math.sqrt(SLABS * NX * NZ * NC * WIDTH))
     turned = total.T
     out[:, :TILE] = turned[:PANEL]
@@ -235,8 +264,10 @@
         core_copy(g).wait_send()
         for d in range(1, NX):
             x_copy(g, d).wait_send()
-        if g < GROUPS - 1:
-            z_copy(g).wait_send()
+
+        @pl.when(z != g)
+        def _():
+            z_copy(g, z_slot(g)).wait_send()
 
     @pl.when(aux == 0)
     def _():
@@ -266,25 +297,27 @@
             pltpu.VMEM((WINDOW, WINDOW), BF16),
             pltpu.VMEM((2, PANEL, SLABS, 128), BF16),
             pltpu.VMEM((WIDTH, 2 * SLABS * PANEL), BF16),
-            pltpu.VMEM((2, SLABS * PAIR, 128), F32),
+            pltpu.VMEM((4, SLABS * PAIR, 128), F32),
             pltpu.VMEM((GROUPS, NX) + piece, F32),
             pltpu.VMEM((GROUPS, NX) + piece, F32),
             pltpu.VMEM((GROUPS, NX) + piece, F32),
             pltpu.VMEM((GROUPS, NX - 1) + piece, BF16),
             pltpu.VMEM((GROUPS, NX - 1) + piece, BF16),
-            pltpu.VMEM((GROUPS - 1,) + piece, BF16),
-            pltpu.VMEM((GROUPS - 1,) + piece, BF16),
+            pltpu.VMEM((GROUPS,) + piece, F32),
+            pltpu.VMEM((GROUPS,) + piece, BF16),
+            pltpu.VMEM((NZ,) + piece, BF16),
             pltpu.SemaphoreType.DMA((GROUPS, 2)),
             pltpu.SemaphoreType.DMA,
             pltpu.SemaphoreType.DMA((2,)),
             pltpu.SemaphoreType.DMA((NAUX - 1, 2)),
             pltpu.SemaphoreType.DMA((2,)),
+            pltpu.SemaphoreType.REGULAR((NZ,)),
             pltpu.SemaphoreType.DMA((GROUPS,)),
             pltpu.SemaphoreType.DMA((GROUPS,)),
             pltpu.SemaphoreType.DMA((GROUPS, NX - 1)),
             pltpu.SemaphoreType.DMA((GROUPS, NX - 1)),
-            pltpu.SemaphoreType.DMA((GROUPS - 1,)),
-            pltpu.SemaphoreType.DMA((GROUPS - 1,)),
+            pltpu.SemaphoreType.DMA((GROUPS,)),
+            pltpu.SemaphoreType.DMA((NZ,)),
         ],
         compiler_params=pltpu.CompilerParams(
             collective_id=0, has_side_effects=True, vmem_limit_bytes=32 << 20

time: 28.2 us -> 26.4 us (0.936)
  the two profiles are of different devices: /device:TPU:16 before, /device:TPU:232 now
where the time goes in v3:
time: 26.4 us
  Pallas kernels  25.7 us (97%)
  local copies, waits for them, and re-layouts  0.62 us (2%)
    pallas_call x1, Pallas kernels, on_device(): pl.pallas_call(kernel, out_shape=jax.ShapeDtypeStruct((PANEL, ROWS), F32)...  25.7 us
    unnamed x1, local copies, waits for them, and re-layouts  0.62 us

profile of v3, /device:TPU:232, one launch (start us, length us, event | category | flops | bytes accessed | tf_op | source)
XLA Modules:
  0.0 26.4 jit_solution(13511811226347020459)
XLA Ops:
  0.0 25.7 %shard_map.46 = f32[64,120]{1,0:T(8,128)S(1)} custom-call(bf16[4,8,240,2,256]{4,3,2,1,0:T(2,128)(2,1)} %bitcast.2, bf16[1,512,512]{2,1,0:T(8,128)(2,1)} %density.1, s32[2,1,4]{2,1,0:T(1,128)} %block_ids_in.1, s32[1,2]{1,0:T(1,128)} %bitcast.3), custom_call_target="tpu_custom_call" | custom-call | tf_op jit(solution)/shard_map/pallas_call | solution.py:282
  25.7 0.6 %copy.6 = f32[64,120]{1,0:T(8,128)} copy(f32[64,120]{1,0:T(8,128)S(1)} %shard_map.46) | data formatting | bytes 61440

commit v4 on v3

--- a/solution.py
+++ b/solution.py
@@ -45,21 +45,22 @@
     z_peer = [{"orb": at(x, of, core)} for of in range(NZ)]
 
     barrier = pltpu.get_barrier_semaphore()
+
+    @pl.when(aux == 0)
+    def _():
+        for d in range(1, NAUX):
+            pl.semaphore_signal(barrier, inc=1, device_id={"aux": d}, device_id_type=pl.DeviceIdType.MESH)
+
+    @pl.when(aux != 0)
+    def _():
+        pl.semaphore_signal(barrier, inc=1, device_id={"aux": 0}, device_id_type=pl.DeviceIdType.MESH)
+
     for peer in [sibling] + x_peer[1:]:
         pl.semaphore_signal(barrier, inc=1, device_id=peer, device_id_type=pl.DeviceIdType.MESH)
     for of in range(1, NZ):
         @pl.when(z < of)
         def _():
             pl.semaphore_signal(barrier, inc=1, device_id=z_peer[of], device_id_type=pl.DeviceIdType.MESH)
-
-    @pl.when(aux == 0)
-    def _():
-        for d in range(1, NAUX):
-            pl.semaphore_signal(barrier, inc=1, device_id={"aux": d}, device_id_type=pl.DeviceIdType.MESH)
-
-    @pl.when(aux != 0)
-    def _():
-        pl.semaphore_signal(barrier, inc=1, device_id={"aux": 0}, device_id_type=pl.DeviceIdType.MESH)
 
     lead_in = [
         pltpu.make_async_copy(
@@ -108,8 +109,8 @@
         pl.semaphore_wait(barrier, 1 + NX - 1 + NAUX - 1 + z)
         for j in range(2):
             lead_in[j].wait()
-        for d in (2, 1, 3):
-            for j in range(2):
+        for j in range(2):
+            for d in (1, 2, 3):
                 lead_copy(d, j).start()
 
     @pl.when(aux != 0)

time: 26.4 us -> 26.3 us (level)
  the two profiles are of different devices: /device:TPU:232 before, /device:TPU:240 now
where the time goes in v4:
time: 26.3 us; the launch traced here: 26.2 us
  Pallas kernels  25.6 us (97%)
  local copies, waits for them, and re-layouts  0.62 us (2%)
    pallas_call x1, Pallas kernels, on_device(): pl.pallas_call(kernel, out_shape=jax.ShapeDtypeStruct((PANEL, ROWS), F32)...  25.6 us
    unnamed x1, local copies, waits for them, and re-layouts  0.62 us

profile of v4, /device:TPU:240, one launch (start us, length us, event | category | flops | bytes accessed | tf_op | source)
XLA Modules:
  0.0 26.2 jit_solution(16206607392077753313)
XLA Ops:
  0.0 25.6 %shard_map.46 = f32[64,120]{1,0:T(8,128)S(1)} custom-call(bf16[4,8,240,2,256]{4,3,2,1,0:T(2,128)(2,1)} %bitcast.2, bf16[1,512,512]{2,1,0:T(8,128)(2,1)} %density.1, s32[2,1,4]{2,1,0:T(1,128)} %block_ids_in.1, s32[1,2]{1,0:T(1,128)} %bitcast.3), custom_call_target="tpu_custom_call" | custom-call | tf_op jit(solution)/shard_map/pallas_call | solution.py:283
  25.6 0.6 %copy.6 = f32[64,120]{1,0:T(8,128)} copy(f32[64,120]{1,0:T(8,128)S(1)} %shard_map.46) | data formatting | bytes 61440

commit v5 on v4

--- a/solution.py
+++ b/solution.py
@@ -230,28 +230,22 @@
     for pair in rows_in:
         for copy in pair:
             copy.wait()
-    for step in range(len(BLOCKS) + C_LAG + X_LAG):
+    for step in range(len(BLOCKS) + C_LAG):
         fresh = BLOCKS[step] if step < len(BLOCKS) else ()
         ripe = BLOCKS[step - C_LAG] if 0 <= step - C_LAG < len(BLOCKS) else ()
         done = BLOCKS[step - C_LAG - X_LAG] if step >= C_LAG + X_LAG else ()
+        for g in fresh:
+            multiply(g)
+            core_copy(g).start()
         for g in ripe:
             core_copy(g).wait_recv()
-        for g in ripe:
             add_sibling(g)
-        if not fresh:
-            for g in ripe:
-                for d in (2, 1, 3):
-                    x_copy(g, d).start()
-        for g in fresh:
-            multiply(g)
-        if fresh:
-            for g in ripe:
-                for d in (2, 1, 3):
-                    x_copy(g, d).start()
-        for g in fresh:
-            core_copy(g).start()
-        for g in done:
+            for d in (2, 1, 3):
+                x_copy(g, d).start()
+        for g in done if fresh else ():
             add_x(g)
+    for g in range(GROUPS - C_LAG - X_LAG, GROUPS):
+        add_x(g)
     total = totals[z]
     for slot in range(NZ - 1):
         z_copy(0, slot).wait_recv()

time: 26.3 us -> 25.8 us (0.981)
  the two profiles are of different devices: /device:TPU:240 before, /device:TPU:16 now
where the time goes in v5:
time: 25.8 us; the launch traced here: 25.5 us
  Pallas kernels  24.9 us (97%)
  local copies, waits for them, and re-layouts  0.62 us (2%)
    pallas_call x1, Pallas kernels, on_device(): pl.pallas_call(kernel, out_shape=jax.ShapeDtypeStruct((PANEL, ROWS), F32)...  24.9 us
    unnamed x1, local copies, waits for them, and re-layouts  0.62 us

profile of v5, /device:TPU:16, one launch (start us, length us, event | category | flops | bytes accessed | tf_op | source)
XLA Modules:
  0.0 25.5 jit_solution(5755025319451884089)
XLA Ops:
  0.0 24.9 %shard_map.46 = f32[64,120]{1,0:T(8,128)S(1)} custom-call(bf16[4,8,240,2,256]{4,3,2,1,0:T(2,128)(2,1)} %bitcast.2, bf16[1,512,512]{2,1,0:T(8,128)(2,1)} %density.1, s32[2,1,4]{2,1,0:T(1,128)} %block_ids_in.1, s32[1,2]{1,0:T(1,128)} %bitcast.3), custom_call_target="tpu_custom_call" | custom-call | tf_op jit(solution)/shard_map/pallas_call | solution.py:277
  24.9 0.6 %copy.6 = f32[64,120]{1,0:T(8,128)} copy(f32[64,120]{1,0:T(8,128)S(1)} %shard_map.46) | data formatting | bytes 61440

commit v6 on v5

--- a/solution.py
+++ b/solution.py
@@ -28,7 +28,7 @@
 
 def kernel(
     tensor, density, block_ids_in, counts_in, out, block_ids, counts, small_sem,
-    rows, dens, lead, weights, product, own, sibling_out, sibling_in, x_out, x_in, totals, z_out, z_in,
+    rows, dens, lead, weights, folded, own, sibling_out, sibling_in, x_out, x_in, totals, z_out, z_in,
     rows_sem, dens_sem, lead_sem, lead_send, lead_recv,
     z_ready, c_send, c_recv, x_send, x_recv, z_send, z_recv,
 ):
@@ -161,6 +161,9 @@
     weights[:, SLABS * PANEL :] = (weight - high.astype(F32)).astype(BF16)
 
     left = lax.broadcasted_iota(jnp.int32, (TILE, 128), 1) < PANEL
+    eights = (SLABS * PAIR // 16, 8, 128)
+    half = lax.broadcasted_iota(jnp.int32, eights, 2) < PANEL
+    even = lax.rem(lax.broadcasted_iota(jnp.int32, eights, 1), 2) == 0
 
     def multiply(g):
         for d in range(NX):
@@ -170,18 +173,16 @@
                 [rows[g, j, x_of].reshape(SLABS * PAIR, 128) for j in range(2)], axis=1
             )
             y = jnp.dot(strip, weights[...], preferred_element_type=F32)
-            product[slot_of] = y[:, :128] + y[:, 128:]
+            v = (y[:, :128] + y[:, 128:]).reshape(SLABS * PAIR // 16, 16, 128)
+            v0, v1 = v[:, :8], v[:, 8:]
+            up, down = pltpu.roll(v0, 7, 1), pltpu.roll(v1, 1, 1)
+            fold = jnp.where(half, jnp.where(even, v0, down), jnp.where(even, up, v1)).reshape(PAIR, 128)
+            folded[slot_of] = fold
             for core_of, dest in ((1 - core, sibling_out), (core, own)):
-                start = core_of * (SLABS * ROWS)
-
-                def every_second(offset):
-                    return product[slot_of, pl.ds(start + offset, TILE, SLABS), :]
-
-                low = [every_second(k) for k in range(SLABS)]
-                top = [every_second(SLABS * SHIFT + k) for k in range(SLABS)]
-                dest[g, d] = jnp.where(left, low[0], top[1]) + pltpu.roll(
-                    jnp.where(left, top[0], low[1]), PANEL, 1
-                )
+                base = core_of * ROWS
+                low = folded[slot_of, pl.ds(base, TILE), :]
+                top = folded[slot_of, pl.ds(base + SHIFT, TILE), :]
+                dest[g, d] = jnp.where(left, low, top) + pltpu.roll(jnp.where(left, top, low), PANEL, 1)
 
     def core_copy(g):
         return pltpu.make_async_remote_copy(
@@ -251,6 +252,10 @@
         z_copy(0, slot).wait_recv()
         total = total + z_in[slot].astype(F32)
     total = total * (1.0 / math.sqrt(SLABS * NX * NZ * NC * WIDTH))
+    folded[0, :TILE] = total
+    total = jnp.concatenate(
+        [folded[0, pl.ds(k, TILE // 2, 2), :].reshape(TILE // 8, 4, 128) for k in range(2)], axis=1
+    ).reshape(TILE, 128)
     turned = total.T
     out[:, :TILE] = turned[:PANEL]
     out[:, TILE:] = turned[PANEL:, TILE - SHIFT :]
@@ -292,7 +297,7 @@
             pltpu.VMEM((WINDOW, WINDOW), BF16),
             pltpu.VMEM((2, PANEL, SLABS, 128), BF16),
             pltpu.VMEM((WIDTH, 2 * SLABS * PANEL), BF16),
-            pltpu.VMEM((4, SLABS * PAIR, 128), F32),
+            pltpu.VMEM((4, PAIR, 128), F32),
             pltpu.VMEM((GROUPS, NX) + piece, F32),
             pltpu.VMEM((GROUPS, NX) + piece, F32),
             pltpu.VMEM((GROUPS, NX) + piece, F32),

time: 25.8 us -> 25.7 us (level)
  no operation moved by 1% of the time
where the time goes in v6:
time: 25.7 us; the launch traced here: 25.5 us
  Pallas kernels  24.9 us (97%)
  local copies, waits for them, and re-layouts  0.62 us (2%)
    pallas_call x1, Pallas kernels, on_device(): pl.pallas_call(kernel, out_shape=jax.ShapeDtypeStruct((PANEL, ROWS), F32)...  24.9 us
    unnamed x1, local copies, waits for them, and re-layouts  0.62 us

profile of v6, /device:TPU:16, one launch (start us, length us, event | category | flops | bytes accessed | tf_op | source)
XLA Modules:
  0.0 25.5 jit_solution(3578482294590603557)
XLA Ops:
  0.0 24.9 %shard_map.46 = f32[64,120]{1,0:T(8,128)S(1)} custom-call(bf16[4,8,240,2,256]{4,3,2,1,0:T(2,128)(2,1)} %bitcast.2, bf16[1,512,512]{2,1,0:T(8,128)(2,1)} %density.1, s32[2,1,4]{2,1,0:T(1,128)} %block_ids_in.1, s32[1,2]{1,0:T(1,128)} %bitcast.3), custom_call_target="tpu_custom_call" | custom-call | tf_op jit(solution)/shard_map/pallas_call | solution.py:282
  24.9 0.6 %copy.6 = f32[64,120]{1,0:T(8,128)} copy(f32[64,120]{1,0:T(8,128)S(1)} %shard_map.46) | data formatting | bytes 61440
